TPU v7x, 512 devices: a whole 4x8x8 slice. The times are simulated.
512 devices in a mesh: inp: 128 (over y, z, core), sec: 4 (over x).
Axes of the slice: x: 4, y: 8, z: 8, core: 2. Of those that a mesh axis runs over, the one named last changes fastest.
Arguments:
- voltages: bfloat16 [2, 2048, 32768], P(None, 'inp', 'sec'), may hold values from -6 to 6
- filter_taps: float32 [4, 1024], replicated, may hold values from -3 to 3
- flagged: int32 [64], replicated, may hold values from 0 to 1023, as said below
- channel_owner: int32 [1024], replicated, may hold values from 0 to 127, as said below
- ref_inputs: int32 [12], replicated, may hold values from 0 to 2047, as said below
Outputs:
- visibilities: float32 [128, 16, 2, 12, 2048], P('inp', None, None, None, 'sec')
Inputs may be any that keep to these rules, and one draw needn't show every extreme that they name: `flagged`: 64 distinct channels. `channel_owner`: no owner has more than 16 channels in all; some owner has exactly 16 unflagged channels. `ref_inputs`: 12 distinct inputs, among them input 0 and input 2048 - 1.
All inputs are finite; a program needn't handle non-finite values.
Results may differ from a plain program's by a relative error of at most 0.004.
Values may be sent and summed in bfloat16 or wider, within the bound.
A program may use at most 64 MiB of HBM per device.

v0:
```python
import math

import jax
import jax.numpy as jnp
from jax import lax
from jax.sharding import PartitionSpec as P

CHANNELS = 1024
TAPS = 4


def passed_along(value, axis, steps):
    count = lax.axis_size(axis)
    first, last = (max(0, -steps), min(count, count - steps))
    return lax.ppermute(value, axis, [(source, source + steps) for source in range(first, last)])


def slot_table(flagged, channel_owner, owners, capacity):
    channel_count = channel_owner.shape[0]
    channel_ids = jnp.arange(channel_count, dtype=jnp.int32)
    dropped = jnp.any(channel_ids[:, None] == flagged[None, :], axis=1)
    member = (
        (channel_owner[:, None] == jnp.arange(owners, dtype=jnp.int32)[None, :])
        & (~dropped)[:, None]
    ).astype(jnp.int32)
    before = jnp.cumsum(member, axis=0) - member
    slot_rank = jnp.sum(before * member, axis=1)
    target = jnp.where(dropped, owners * capacity, channel_owner * capacity + slot_rank)
    table = jnp.full((owners * capacity + 1,), -1, jnp.int32).at[target].set(channel_ids)
    return table[: owners * capacity]


def cross_products(slot_data, ref_data, block_total):
    slot_count = slot_data.shape[0]
    input_count = slot_data.shape[3]
    stacked_rows = 2 * slot_data.shape[2]
    rotated = jnp.stack([-ref_data[:, 1], ref_data[:, 0]], axis=1)
    weights_left = jnp.concatenate([ref_data, rotated], axis=3).reshape(
        slot_count, stacked_rows, -1
    )
    right_side = slot_data.reshape(slot_count, stacked_rows, input_count)
    product = jnp.einsum(
        "kcr,kci->kri", weights_left, right_side, preferred_element_type=jnp.float32
    )
    return (product / block_total).reshape(slot_count, 2, -1, input_count)


def on_device(voltages, filter_taps, flagged, channel_owner, ref_inputs):
    owners = lax.axis_size("inp")
    sections = lax.axis_size("sec")
    capacity = 2 * CHANNELS // owners
    local_inputs = voltages.shape[1]
    local_blocks = voltages.shape[2] // CHANNELS
    block_total = local_blocks * sections
    frames = voltages.reshape(2, local_inputs, local_blocks, CHANNELS)
    frames_ahead = passed_along(frames[:, :, : TAPS - 1], "sec", -1)
    extended = jnp.concatenate([frames, frames_ahead], axis=2)
    filtered = jnp.zeros(frames.shape, jnp.float32)
    for tap_index in range(TAPS):
        filtered = filtered + filter_taps[tap_index] * extended[
            :, :, tap_index : tap_index + local_blocks
        ].astype(jnp.float32)
    per_part = local_blocks * local_inputs
    ordered = jnp.transpose(filtered, (0, 2, 1, 3)).reshape(2 * per_part, CHANNELS)
    indices = jnp.arange(CHANNELS, dtype=jnp.int32)
    phases = indices[:, None] * indices[None, :] % CHANNELS
    angles = phases.astype(jnp.float32) * (2.0 * math.pi / CHANNELS)
    table_both = jnp.concatenate([jnp.cos(angles), jnp.sin(angles)], axis=1)
    product = lax.dot_general(
        table_both,
        ordered,
        (((0,), (1,)), ((), ())),
        precision=lax.Precision.HIGHEST,
        preferred_element_type=jnp.float32,
    )
    scaling = 1.0 / math.sqrt(CHANNELS)
    real_part = (product[:CHANNELS, :per_part] + product[CHANNELS:, per_part:]) * scaling
    imag_part = (product[:CHANNELS, per_part:] - product[CHANNELS:, :per_part]) * scaling
    spectra = jnp.stack([real_part, imag_part], axis=1).astype(jnp.bfloat16)
    slot_channel = slot_table(flagged, channel_owner, owners, capacity)
    picked = spectra[jnp.maximum(slot_channel, 0)]
    send_buffer = picked.reshape(owners, capacity, 2, local_blocks, local_inputs).transpose(
        1, 2, 3, 0, 4
    )
    send_buffer = send_buffer.reshape(capacity, 2, local_blocks, owners * local_inputs)
    mine = lax.dynamic_slice_in_dim(slot_channel, lax.axis_index("inp") * capacity, capacity)
    occupied = (mine >= 0).astype(jnp.float32)[:, None, None, None]
    regrouped = lax.all_to_all(
        lax.all_to_all(send_buffer, "inp", split_axis=3, concat_axis=3, tiled=True),
        "sec",
        split_axis=3,
        concat_axis=2,
        tiled=True,
    )
    quarter = regrouped.shape[3]
    offset = ref_inputs - lax.axis_index("sec") * quarter
    inside = ((offset >= 0) & (offset < quarter)).astype(jnp.float32)
    local_refs = (
        jnp.take(regrouped, jnp.clip(offset, 0, quarter - 1), axis=3).astype(jnp.float32) * inside
    )
    ref_data = lax.psum(local_refs.astype(jnp.bfloat16), "sec")
    summed = cross_products(regrouped, ref_data, block_total)
    return (summed * occupied)[None]


def solution(mesh):
    return jax.shard_map(
        on_device,
        mesh=mesh,
        in_specs=(P(None, "inp", "sec"), P(), P(), P(), P()),
        out_specs=P("inp", None, None, None, "sec"),
        check_vma=False,
    )
```

profile of v0, /device:TPU:24, one launch (start us, length us, event | category | flops | bytes accessed | tf_op | source)
XLA Modules:
  0.0 223.1 jit_solution(9045765449512700308)
XLA Ops:
  0.0 1.3 copy.88
  1.3 0.1 slice.72
  1.4 0.0 copy-start.4
  1.4 0.0 copy-start.2
  1.4 0.0 copy-start.1
  1.5 1.4 collective-permute-start
  2.9 17.5 %fusion.10 = (f32[1024,1024]{1,0:T(8,128)}, f32[1024,1024]{1,0:T(8,128)}) fusion(), kind=kLoop, calls=%fused_computation.16 | loop fusion | flops 14680064 | bytes 8388608 | tf_op jit(solution)/shard_map/sin | solution.py:68
  20.4 0.0 copy-done.4
  20.4 0.1 fusion.26
  20.5 0.1 copy.72
  20.7 0.0 copy-done.2
  20.7 0.0 copy-done.1
  20.7 0.1 copy.71
  20.8 0.3 fusion.18
  21.2 0.1 copy.73
  21.4 0.5 fusion.17
  21.9 4.5 %scatter_custom_fusion = s32[2049]{0:T(1024)S(1)} fusion(s32[1024]{0:T(1024)S(1)} %compare_select_fusion, s32[1024]{0:T(1024)S(1)} %iota.19, s32[]{:T(128)} %constant.34.clone.1), kind=kCustom, calls=%fused_computation.50 | custom fusion | bytes 8200 | tf_op jit(solution)/shard_map/scatter | solution.py:29
  26.5 0.0 copy-start
  26.5 0.0 collective-permute-done
  26.5 0.2 constant_dynamic-update-slice_fusion
  26.7 0.6 add_bitcast_fusion
  27.2 0.6 copy.70
  27.9 0.8 copy-done
  28.6 16.3 %fusion = f32[2048,256]{1,0:T(8,128)S(1)} fusion(f32[256,1024]{1,0:T(8,128)S(1)} %bitcast.66, f32[1024,1024]{1,0:T(8,128)S(1)} %copy-done, f32[1024,1024]{1,0:T(8,128)} %get-tuple-element.23), kind=kOutput, calls=%fused_computation.3 | convolution fusion | flops 6444548096 | bytes 11534336 | tf_op jit(solution)/shard_map/dot_general | solution.py:69
  45.0 0.1 fusion.23
  45.1 0.1 pad_maximum_fusion
  45.1 0.5 copy.74
  45.7 7.0 %gather_fusion = bf16[2048,2,128]{2,1,0:T(2,128)(2,1)S(1)} fusion(bf16[1024,2,128]{2,1,0:T(2,128)(2,1)S(1)} %copy.74, s32[2048]{0:T(1024)S(1)} %get-tuple-element.18), kind=kCustom, calls=%fused_computation | custom fusion | bytes 2105344 | tf_op jit(solution)/shard_map/gather | solution.py:81
  52.7 0.1 copy.75
  52.9 7.3 %reshape.73 = bf16[128,16,2,8,16]{4,3,1,0,2:T(8,128)(2,1)} reshape(bf16[2048,2,128]{2,0,1:T(8,128)(2,1)S(1)} %copy.75) | data formatting | bytes 2097152 | tf_op jit(solution)/shard_map/reshape | solution.py:82
  60.2 13.9 %copy.85 = bf16[16,2,8,128,16]{0,2,1,4,3:T(8,128)(2,1)} copy(bf16[16,2,8,128,16]{4,2,0,3,1:T(8,128)(2,1)} %bitcast.57) | data formatting | bytes 2097152 | tf_op jit(solution)/shard_map/reshape | solution.py:85
  74.1 11.7 %reshape.107 = bf16[128,2,2048]{2,1,0:T(2,128)(2,1)S(1)} reshape(bf16[2048,2,8,16]{3,2,1,0:T(8,128)(2,1)} %bitcast.58) | data formatting | bytes 2097152
  85.8 45.7 %all_to_all.23 = bf16[128,2,2048]{2,1,0:T(2,128)(2,1)S(1)} all-to-all(bf16[128,2,2048]{2,1,0:T(2,128)(2,1)S(1)} %reshape.107), channel_id=1, replica_groups=mesh['inp'=128,'sec'=4] {'inp'}, dimensions={0} | all-to-all | bytes 2097152 | tf_op jit(solution)/shard_map/all_to_all | solution.py:89
  131.5 7.5 %reshape.108 = bf16[2048,2,8,16]{3,2,1,0:T(8,128)(2,1)} reshape(bf16[128,2,2048]{2,1,0:T(2,128)(2,1)S(1)} %all_to_all.23) | data formatting | bytes 2097152
  139.1 7.5 %bitcast_bitcast_fusion = bf16[2048,2,8,16]{3,2,1,0:T(8,128)(2,1)} fusion(bf16[2048,2,8,16]{3,2,1,0:T(8,128)(2,1)} %reshape.108), kind=kLoop, calls=%fused_computation.67 | loop fusion | bytes 2097152
  146.5 0.0 copy-start.3
  146.5 11.0 %reshape.109 = bf16[4,2,65536]{2,1,0:T(2,128)(2,1)} reshape(bf16[2048,2,8,16]{3,2,1,0:T(8,128)(2,1)} %bitcast_bitcast_fusion) | data formatting | bytes 2097152
  157.5 5.5 %all-to-all-start.1 = ((bf16[4,2,65536]{2,1,0:T(2,128)(2,1)}), bf16[4,2,65536]{2,1,0:T(2,128)(2,1)S(1)}, u32[]{:S(2)}, u32[]{:S(2)}) async-start(bf16[4,2,65536]{2,1,0:T(2,128)(2,1)} %reshape.109), calls=%async_computation.1 | async-start | bytes 2097152 | tf_op jit(solution)/shard_map/all_to_all | solution.py:88
  163.0 0.1 compare_convert_fusion
  163.0 0.0 copy-done.3
  163.1 16.3 %all-to-all-done.1 = bf16[4,2,65536]{2,1,0:T(2,128)(2,1)S(1)} async-done(((bf16[4,2,65536]{2,1,0:T(2,128)(2,1)}), bf16[4,2,65536]{2,1,0:T(2,128)(2,1)S(1)}, u32[]{:S(2)}, u32[]{:S(2)}) %all-to-all-start.1) | async-done | bytes 1048608 | tf_op jit(solution)/shard_map/all_to_all | solution.py:88
  179.4 7.1 %reshape.110 = bf16[2048,2,8,16]{3,2,1,0:T(8,128)(2,1)} reshape(bf16[4,2,65536]{2,1,0:T(2,128)(2,1)S(1)} %all-to-all-done.1) | data formatting | bytes 2097152
  186.5 9.4 %copy.86 = bf16[16,2,8,4,512]{4,3,2,1,0:T(4,128)(2,1)S(1)} copy(bf16[16,2,8,4,512]{0,2,1,4,3:T(8,128)(2,1)} %bitcast.56) | data formatting | bytes 2097152 | tf_op jit(solution)/shard_map/all_to_all | solution.py:88
  195.9 0.3 copy.91
  196.1 4.7 %copy.80 = bf16[16,2,32,512]{2,0,3,1:T(8,128)(2,1)} copy(bf16[16,2,32,512]{3,2,1,0:T(8,128)(2,1)S(1)} %bitcast.59) | data formatting | bytes 2097152 | tf_op jit(solution)/shard_map/all_to_all | solution.py:88
  200.9 2.8 %gather_fusion.1 = bf16[12,16,2,32]{3,1,2,0:T(8,128)(2,1)S(1)} fusion(bf16[16,2,32,512]{2,0,3,1:T(8,128)(2,1)} %copy.80, s32[1024]{0:T(1024)S(1)} %pad_clamp_fusion), kind=kCustom, calls=%fused_computation.1 | custom fusion | bytes 49200 | tf_op jit(solution)/shard_map/jit(_take)/gather | solution.py:99
  203.6 0.1 fusion.28
  203.7 16.6 %psum.7 = bf16[16,2,32,12]{2,0,1,3:T(8,128)(2,1)S(1)} all-reduce(bf16[16,2,32,12]{2,0,1,3:T(8,128)(2,1)S(1)} %fusion.28), channel_id=1, replica_groups=mesh['inp'=128,'sec'=4] {'sec'}, use_global_device_ids=true, to_apply=%region_5.6 | all-reduce | flops 12288 | bytes 49152 | tf_op jit(solution)/shard_map/psum | solution.py:101
  220.4 0.2 copy.81
  220.6 0.1 reshape.75
  220.7 0.3 convolution_multiply_fusion
  221.0 0.5 copy.83
  221.4 0.2 broadcast_multiply_fusion
  221.6 1.5 copy.84
  (14 shorter events, 0.2 us)
Async XLA Ops:
  1.4 19.0 %copy-start.4 = (s32[64]{0:T(128)S(1)}, s32[64]{0:T(128)}, u32[]{:S(2)}) copy-start(s32[64]{0:T(128)} %param.7) | copy-start | bytes 772
  1.4 19.2 %copy-start.2 = (f32[4,1024]{1,0:T(4,128)S(1)}, f32[4,1024]{1,0:T(4,128)}, u32[]{:S(2)}) copy-start(f32[4,1024]{1,0:T(4,128)} %param.6) | copy-start | bytes 49156
  1.4 19.3 %copy-start.1 = (s32[1024]{0:T(1024)S(1)}, s32[1024]{0:T(1024)}, u32[]{:S(2)}) copy-start(s32[1024]{0:T(1024)} %param.8) | copy-start | bytes 12292
  1.5 25.0 %collective-permute-start = (bf16[2,16,3,1024]{3,2,1,0:T(4,128)(2,1)S(1)}, bf16[2,16,3,1024]{3,2,1,0:T(4,128)(2,1)S(1)}, u32[]{:S(2)}, u32[]{:S(2)}) collective-permute-start(bf16[2,16,3,1024]{3,2,1,0:T(4,128)(2,1)S(1)} %slice.72), channel_id=1, source_target_pairs={{1,0},{2,1},{3,2},{5,4},{6,5},{7,6},{9,8},{10,9},{11,10},{13,12},{... | collective-permute-start | bytes 589832 | tf_op jit(solution)/shard_map/ppermute | solution.py:15
  26.5 2.2 copy-start
  146.5 16.5 %copy-start.3 = (s32[12]{0:T(128)S(1)}, s32[12]{0:T(128)}, u32[]{:S(2)}) copy-start(s32[12]{0:T(128)} %param.9) | copy-start | bytes 148
  157.5 21.9 %all-to-all-start.1 = ((bf16[4,2,65536]{2,1,0:T(2,128)(2,1)}), bf16[4,2,65536]{2,1,0:T(2,128)(2,1)S(1)}, u32[]{:S(2)}, u32[]{:S(2)}) async-start(bf16[4,2,65536]{2,1,0:T(2,128)(2,1)} %reshape.109), calls=%async_computation.1 | async-start | bytes 2097152 | tf_op jit(solution)/shard_map/all_to_all | solution.py:88
where the time goes:
time: 224 us; the launch traced here: 223 us
  local copies, waits for them, and re-layouts  101 us (45%)
  blocking collectives  62.3 us (28%)
  other arithmetic  19.7 us (9%)
  matrix products  16.6 us (7%)
  waiting for transfers between devices  16.3 us (7%)
  starting transfers between devices  6.91 us (3%)
    unnamed x17, local copies, waits for them, and re-layouts  46.9 us
    all_to_all x1, blocking collectives, on_device(): lax.all_to_all(send_buffer, 'inp', split_axis=3, concat_axis=3, tiled=True)  45.7 us
    sin x1, other arithmetic, on_device(): table_both = jnp.concatenate([jnp.cos(angles), jnp.sin(angles)], axis=1)  17.5 us
    psum x1, blocking collectives, on_device(): ref_data = lax.psum(local_refs.astype(jnp.bfloat16), 'sec')  16.6 us
    dot_general x1, matrix products, on_device(): lax.dot_general(table_both, ordered, (((0,), (1,)), ((), ())), precision=...  16.3 us
    all_to_all x1, waiting for transfers between devices, on_device(): lax.all_to_all(lax.all_to_all(send_buffer, 'inp', split_axis=3, concat_ax...  16.3 us
    all_to_all x3, local copies, waits for them, and re-layouts, on_device(): lax.all_to_all(lax.all_to_all(send_buffer, 'inp', split_axis=3, concat_ax...  14.4 us
    reshape x1, local copies, waits for them, and re-layouts, on_device(): send_buffer.reshape(capacity, 2, local_blocks, owners * local_inputs)  13.9 us
  transfers between devices with their start and end apart: 2, of which 1 were waited for; matrix products, arithmetic and copies ran while one was open for 11% of the time, Pallas kernels for 0%

commit v1 on v0

v1 whole, which is shorter than its diff:
```python
import functools
import math

import jax
import jax.numpy as jnp
import numpy as np
from jax import lax
from jax.experimental import pallas as pl
from jax.experimental.pallas import tpu as pltpu
from jax.sharding import PartitionSpec as P

CHANNELS = 1024
TAPS = 4
RADIX = 4
SHORT = CHANNELS // RADIX
CAPACITY = 16
LOCAL = 16
HALF = 4
LANES = 128
GROUP = LANES // CAPACITY
REF_ROWS = 16
MESH = pl.DeviceIdType.MESH


def tables():
    n = np.arange(SHORT)
    angle = 2.0 * math.pi * ((n[:, None] * n[None, :]) % SHORT) / SHORT
    cos, sin = np.cos(angle), np.sin(angle)
    full = np.block([[cos, -sin], [sin, cos]]) / math.sqrt(CHANNELS)
    high = full.astype(np.float32).astype(jnp.bfloat16)
    low = (full - high.astype(np.float64)).astype(np.float32).astype(jnp.bfloat16)
    turn = 2.0 * math.pi * np.arange(RADIX)[:, None] * n[None, :] / CHANNELS
    twiddle = np.stack([np.cos(turn), np.sin(turn)], axis=1).reshape(2 * RADIX, SHORT)
    return high, low, twiddle.astype(np.float32)


def kernel(owners, sections, volt, taps, target, refs, high, low, twiddle, out,
           halo, zhi, zlo, stage, onehot, outbox, inbox, refbox, refin, weights,
           halo_sem, send_sem, recv_sem, ref_send, ref_recv):
    p, s = lax.axis_index("inp"), lax.axis_index("sec")
    span = owners // sections
    q = lax.div(p, span)
    place = lax.rem(p, span)
    own_group = lax.div(p, GROUP)
    groups = owners // GROUP
    rows = span * LOCAL
    at_home = q == s

    barrier = pltpu.get_barrier_semaphore()

    def greet(k, carry):
        there_p = s * span + lax.rem(k, span)
        there_s = lax.div(k, span)

        @pl.when(jnp.logical_not((there_p == p) & (there_s == s)))
        def _():
            pl.semaphore_signal(barrier, inc=1, device_id=(there_p, there_s), device_id_type=MESH)
        return carry
    lax.fori_loop(0, owners, greet, 0)
    for d in range(1, sections):
        pl.semaphore_signal(barrier, inc=1, device_id=(p, lax.rem(s + d, sections)), device_id_type=MESH)

    lane = lax.broadcasted_iota(jnp.int32, (LOCAL, LANES), 1)
    block = lane // CAPACITY

    def spectra(h):
        for b in range(HALF):
            parts = []
            for part in range(2):
                pieces = []
                for n1 in range(RADIX):
                    total = None
                    for t in range(TAPS):
                        frame = h * HALF + b + t
                        if frame < 2 * HALF:
                            source = volt[part, :, pl.ds(frame * CHANNELS + n1 * SHORT, SHORT)].astype(jnp.float32)
                        else:
                            source = halo[part, :, pl.ds((frame - 2 * HALF) * CHANNELS + n1 * SHORT, SHORT)].astype(jnp.float32)
                            source = jnp.where(s == sections - 1, 0.0, source)
                        term = taps[t:t + 1, n1 * SHORT:(n1 + 1) * SHORT] * source
                        total = term if total is None else total + term
                    pieces.append(total)
                parts.append(pieces)
            (r0, r1, r2, r3), (i0, i1, i2, i3) = parts
            ar, ai, br, bi = r0 + r2, i0 + i2, r0 - r2, i0 - i2
            cr, ci, dr, di = r1 + r3, i1 + i3, r1 - r3, i1 - i3
            mixed = [(ar + cr, ai + ci), (br + di, bi - dr), (ar - cr, ai - ci), (br - di, bi + dr)]
            for c1 in range(RADIX):
                re, im = mixed[c1]
                if c1:
                    cos, sin = twiddle[2 * c1:2 * c1 + 1, :], twiddle[2 * c1 + 1:2 * c1 + 2, :]
                    re, im = re * cos + im * sin, im * cos - re * sin
                at = pl.ds((c1 * HALF + b) * LOCAL, LOCAL)
                for k, value in enumerate((re, im)):
                    top = value.astype(jnp.bfloat16)
                    zhi[at, k * SHORT:(k + 1) * SHORT] = top
                    zlo[at, k * SHORT:(k + 1) * SHORT] = (value - top.astype(jnp.float32)).astype(jnp.bfloat16)
        top = zhi[...]
        product = jnp.dot(top, high[...], preferred_element_type=jnp.float32)
        product += jnp.dot(zlo[...], high[...], preferred_element_type=jnp.float32)
        product += jnp.dot(top, low[...], preferred_element_type=jnp.float32)
        product = product.astype(jnp.bfloat16)
        deep = HALF * LOCAL
        for c1 in range(RADIX):
            for part in range(2):
                stage[h, part * deep:(part + 1) * deep, c1 * SHORT:(c1 + 1) * SHORT] = (
                    product[c1 * deep:(c1 + 1) * deep, part * SHORT:(part + 1) * SHORT])

    def build(j, carry):
        base = pl.multiple_of(j * LANES, LANES)
        slot = lax.broadcasted_iota(jnp.int32, (SHORT, LANES), 1) + j * LANES
        for c1 in range(RADIX):
            hit = target[:, c1:c1 + 1] == slot
            onehot[c1 * SHORT:(c1 + 1) * SHORT, pl.ds(base, LANES)] = jnp.where(hit, 1.0, 0.0).astype(jnp.bfloat16)
        return carry

    def ship(h):
        def one_group(j, carry):
            g = lax.rem(own_group + j, groups)
            base = pl.multiple_of(g * LANES, LANES)
            picked = jnp.dot(stage[h], onehot[:, pl.ds(base, LANES)], preferred_element_type=jnp.float32)
            tiles = []
            for k in range(GROUP):
                tile = picked[k * LOCAL:(k + 1) * LOCAL, :]
                tiles.append(pltpu.roll(tile, k * CAPACITY, 1) if k else tile)
            for bit in range(3):
                step = 1 << bit
                taken = ((block // step) % 2) == 1
                tiles = [jnp.where(taken, tiles[(m + step) % GROUP], tiles[m]) for m in range(GROUP)]
            for k in range(GROUP):
                outbox[h, g * GROUP + k] = tiles[(GROUP - k) % GROUP].astype(jnp.bfloat16)
            for k in range(GROUP):
                o = g * GROUP + k
                landing = inbox.at[h, s, pl.ds(pl.multiple_of(place * LOCAL, LOCAL), LOCAL), :]
                mine = (o == p) & at_home

                @pl.when(mine)
                def _():
                    pltpu.make_async_copy(outbox.at[h, o], landing, recv_sem.at[h]).start()

                @pl.when(jnp.logical_not(mine))
                def _():
                    pltpu.make_async_remote_copy(
                        src_ref=outbox.at[h, o], dst_ref=landing, send_sem=send_sem.at[h],
                        recv_sem=recv_sem.at[h], device_id=(o, q), device_id_type=MESH).start()
            return carry
        lax.fori_loop(0, groups, one_group, 0)

    lax.fori_loop(0, groups, build, 0)
    spectra(0)

    @pl.when(at_home)
    def _():
        pl.semaphore_wait(barrier, owners - 1 + sections - 1)

    @pl.when(jnp.logical_not(at_home))
    def _():
        pl.semaphore_wait(barrier, owners + sections - 1)

    halo_copy = pltpu.make_async_remote_copy(
        src_ref=volt.at[:, :, pl.ds(0, (TAPS - 1) * CHANNELS)], dst_ref=halo, send_sem=halo_sem.at[0],
        recv_sem=halo_sem.at[1], device_id=(p, lax.rem(s + sections - 1, sections)), device_id_type=MESH)
    halo_copy.start()
    ship(0)
    halo_copy.wait()
    spectra(1)
    ship(1)

    index = lax.broadcasted_iota(jnp.int32, (REF_ROWS, rows), 1) + s * rows
    chosen = jnp.where(refs[...] == index, 1.0, 0.0).astype(jnp.bfloat16)

    def gather_refs(h):
        pltpu.make_async_copy(inbox.at[h], inbox.at[h], recv_sem.at[h]).wait()
        for t in range(sections):
            found = jnp.dot(chosen, inbox[h, t], preferred_element_type=jnp.float32)
            refbox[h, t * REF_ROWS:(t + 1) * REF_ROWS, :] = found.astype(jnp.bfloat16)
        copies = []
        for d in range(1, sections):
            copies.append(pltpu.make_async_remote_copy(
                src_ref=refbox.at[h], dst_ref=refin.at[h, d - 1], send_sem=ref_send.at[h, d - 1],
                recv_sem=ref_recv.at[h, d - 1], device_id=(p, lax.rem(s + d, sections)), device_id_type=MESH))
        for copy in copies:
            copy.start()
        return copies

    wide = lax.broadcasted_iota(jnp.int32, (REF_ROWS, LANES), 1)
    inner = wide % CAPACITY
    part_of = ((wide // CAPACITY + (GROUP - lax.rem(p, GROUP))) % GROUP) // HALF
    sign = jnp.where(part_of == 1, 1.0, -1.0)

    def correlate(h, copies):
        for copy in copies:
            copy.wait()
        total = None
        for t in range(sections):
            at = pl.ds(t * REF_ROWS, REF_ROWS)
            found = refbox[h, at, :].astype(jnp.float32)
            for d in range(1, sections):
                found += refin[h, d - 1, at, :].astype(jnp.float32)
            turned = pltpu.roll(found, LANES // 2, 1) * sign
            for k in range(CAPACITY):
                keep = inner == k
                weights[2 * k * REF_ROWS:(2 * k + 1) * REF_ROWS, t * LANES:(t + 1) * LANES] = (
                    jnp.where(keep, found, 0.0).astype(jnp.bfloat16))
                weights[(2 * k + 1) * REF_ROWS:(2 * k + 2) * REF_ROWS, t * LANES:(t + 1) * LANES] = (
                    jnp.where(keep, turned, 0.0).astype(jnp.bfloat16))
            term = lax.dot_general(weights[:, t * LANES:(t + 1) * LANES], inbox[h, t],
                                   (((1,), (1,)), ((), ())), preferred_element_type=jnp.float32)
            total = term if total is None else total + term
        return total

    first = gather_refs(0)
    total = correlate(0, first)
    second = gather_refs(1)
    total = total + correlate(1, second)
    total = total * (1.0 / (2 * HALF * sections))
    width = out.shape[3]
    for k in range(CAPACITY):
        for part in range(2):
            at = (2 * k + part) * REF_ROWS
            out[0, k, part] = total[at:at + width, :]

    for h in range(2):
        @pl.when(at_home)
        def _():
            some = outbox.at[h, pl.ds(0, owners - 1)]
            pltpu.make_async_copy(some, some, send_sem.at[h]).wait()

        @pl.when(jnp.logical_not(at_home))
        def _():
            pltpu.make_async_copy(outbox.at[h], outbox.at[h], send_sem.at[h]).wait()


def slot_targets(flagged, channel_owner):
    channel = jnp.arange(CHANNELS, dtype=jnp.int32)
    dropped = jnp.any(channel[:, None] == flagged[None, :], axis=1)
    kept_owner = jnp.where(dropped, -1, channel_owner)
    earlier = (kept_owner[None, :] == channel_owner[:, None]) & (channel[None, :] < channel[:, None])
    rank = jnp.sum(earlier.astype(jnp.int32), axis=1)
    return jnp.where(dropped, -1, channel_owner * CAPACITY + rank)


def on_device(voltages, filter_taps, flagged, channel_owner, ref_inputs):
    owners = lax.axis_size("inp")
    sections = lax.axis_size("sec")
    count = ref_inputs.shape[0]
    target = slot_targets(flagged, channel_owner).reshape(SHORT, RADIX)
    refs = jnp.full((REF_ROWS, 1), -1, jnp.int32).at[:count, 0].set(ref_inputs)
    high, low, twiddle = tables()
    inputs = owners * LOCAL // sections
    bf16, f32 = jnp.bfloat16, jnp.float32
    vmem = pl.BlockSpec(memory_space=pltpu.VMEM)
    return pl.pallas_call(
        functools.partial(kernel, owners, sections),
        out_shape=jax.ShapeDtypeStruct((1, CAPACITY, 2, count, inputs), f32),
        in_specs=[vmem] * 7,
        out_specs=vmem,
        scratch_shapes=[
            pltpu.VMEM((2, LOCAL, (TAPS - 1) * CHANNELS), bf16),
            pltpu.VMEM((RADIX * HALF * LOCAL, 2 * SHORT), bf16),
            pltpu.VMEM((RADIX * HALF * LOCAL, 2 * SHORT), bf16),
            pltpu.VMEM((2, 2 * HALF * LOCAL, CHANNELS), bf16),
            pltpu.VMEM((CHANNELS, owners * CAPACITY), bf16),
            pltpu.VMEM((2, owners, LOCAL, LANES), bf16),
            pltpu.VMEM((2, sections, inputs, LANES), bf16),
            pltpu.VMEM((2, sections * REF_ROWS, LANES), bf16),
            pltpu.VMEM((2, sections - 1, sections * REF_ROWS, LANES), bf16),
            pltpu.VMEM((CAPACITY * 2 * REF_ROWS, sections * LANES), bf16),
            pltpu.SemaphoreType.DMA((2,)),
            pltpu.SemaphoreType.DMA((2,)),
            pltpu.SemaphoreType.DMA((2,)),
            pltpu.SemaphoreType.DMA((2, sections - 1)),
            pltpu.SemaphoreType.DMA((2, sections - 1)),
        ],
        compiler_params=pltpu.CompilerParams(
            collective_id=0, has_side_effects=True, vmem_limit_bytes=48 * 1024 * 1024),
    )(voltages, filter_taps, target, refs, jnp.asarray(high), jnp.asarray(low), jnp.asarray(twiddle))


def solution(mesh):
    return jax.shard_map(
        on_device,
        mesh=mesh,
        in_specs=(P(None, "inp", "sec"), P(), P(), P(), P()),
        out_specs=P("inp", None, None, None, "sec"),
        check_vma=False,
    )
```

time: 224 us -> 63.7 us (0.28)
  the two profiles are of different devices: /device:TPU:24 before, /device:TPU:1 now
where the time goes in v1:
time: 63.7 us; the launch traced here: 62.5 us
  Pallas kernels  52.2 us (82%)
  local copies, waits for them, and re-layouts  6.91 us (11%)
  other arithmetic  3.36 us (5%)
    pallas_call x1, Pallas kernels, on_device(): pl.pallas_call(functools.partial(kernel, owners, sections), out_shape=jax...  52.2 us
    unnamed x10, local copies, waits for them, and re-layouts  4.53 us
    pallas_call x1, local copies, waits for them, and re-layouts, on_device(): pl.pallas_call(functools.partial(kernel, owners, sections), out_shape=jax...  1.49 us

profile of v1, /device:TPU:1, one launch (start us, length us, event | category | flops | bytes accessed | tf_op | source)
XLA Modules:
  0.0 62.5 jit_solution(197392231931039895)
XLA Ops:
  0.0 0.8 %fusion.1 = pred[1024]{0:T(1024)(128)(4,1)S(1)} fusion(s32[64]{0:T(128)} %param.12), kind=kLoop, calls=%fused_computation.4 | loop fusion | flops 130048 | bytes 1280 | tf_op jit(solution)/shard_map/reduce_or | solution.py:236
  0.8 0.7 %broadcast_select_fusion = s32[1024]{0:T(1024)S(1)} fusion(pred[1024]{0:T(1024)(128)(4,1)S(1)} %fusion.1, s32[1024]{0:T(1024)} %param.13), kind=kLoop, calls=%fused_computation.6 | loop fusion | flops 1024 | bytes 9216 | tf_op jit(solution)/shard_map/jit(_where)/select_n | solution.py:237
  1.5 1.2 %convert_reduce_fusion = s32[1024]{0:T(1024)S(1)} fusion(s32[1024]{0:T(1024)S(1)} %broadcast_select_fusion, s32[1024]{0:T(1024)} %param.13), kind=kLoop, calls=%fused_computation | loop fusion | flops 5241856 | bytes 12288 | tf_op jit(solution)/shard_map/reduce_sum | solution.py:239
  2.7 0.7 %add_select_fusion = s32[1024]{0:T(1024)S(1)} fusion(pred[1024]{0:T(1024)(128)(4,1)S(1)} %fusion.1, s32[1024]{0:T(1024)S(1)} %convert_reduce_fusion, s32[1024]{0:T(1024)} %param.13), kind=kLoop, calls=%fused_computation.5 | loop fusion | flops 3072 | bytes 13312 | tf_op jit(solution)/shard_map/jit(_where)/select_n | solution.py:240
  3.4 0.7 %copy.13 = s32[12,1]{1,0:T(8,128)S(1)} copy(s32[12,1]{0,1:T(1,128)} %bitcast.1) | data formatting | bytes 96 | tf_op jit(solution)/shard_map/reshape.28
  4.1 0.1 reshape.36.target
  4.3 0.0 copy-start
  4.3 1.0 %copy-done = bf16[2,16,8192]{2,1,0:T(8,128)(2,1)S(1)} copy-done((bf16[2,16,8192]{2,1,0:T(8,128)(2,1)S(1)}, bf16[2,16,8192]{2,1,0:T(8,128)(2,1)}, u32[]{:S(2)}) %copy-start) | copy-done | bytes 524312
  5.3 0.0 copy-start.1
  5.3 1.0 %copy-done.1 = bf16[512,512]{1,0:T(8,128)(2,1)S(1)} copy-done((bf16[512,512]{1,0:T(8,128)(2,1)S(1)}, bf16[512,512]{1,0:T(8,128)(2,1)}, u32[]{:S(2)}) %copy-start.1) | copy-done | bytes 524312
  6.3 0.0 copy-start.2
  6.3 1.0 %copy-done.2 = bf16[512,512]{1,0:T(8,128)(2,1)S(1)} copy-done((bf16[512,512]{1,0:T(8,128)(2,1)S(1)}, bf16[512,512]{1,0:T(8,128)(2,1)}, u32[]{:S(2)}) %copy-start.2) | copy-done | bytes 524312
  7.4 0.0 copy-start.3
  7.4 0.7 %copy-done.3 = f32[4,1024]{1,0:T(4,128)S(1)} copy-done((f32[4,1024]{1,0:T(4,128)S(1)}, f32[4,1024]{1,0:T(4,128)}, u32[]{:S(2)}) %copy-start.3) | copy-done | bytes 16408
  8.1 0.0 copy-start.4
  8.1 0.7 %copy-done.4 = f32[8,256]{1,0:T(8,128)S(1)} copy-done((f32[8,256]{1,0:T(8,128)S(1)}, f32[8,256]{1,0:T(8,128)}, u32[]{:S(2)}) %copy-start.4) | copy-done | bytes 8216
  8.8 52.2 %shard_map.82 = f32[1,16,2,12,512]{4,3,2,1,0:T(8,128)S(1)} custom-call(bf16[2,16,8192]{2,1,0:T(8,128)(2,1)S(1)} %copy-done, f32[4,1024]{1,0:T(4,128)S(1)} %copy-done.3, s32[256,4]{1,0:T(8,128)S(1)} %reshape.36.target, s32[16,1]{1,0:T(8,128)S(1)} %scatter.4.refs, bf16[512,512]{1,0:T(8,128)(2,1)S(1)} %copy-done.2, bf16[512,512]{1,0:T(8,128)(2,1)S(1)} %copy-done.1, ...), custom_call_target="tpu_custom_call" | custom-call | tf_op jit(solution)/shard_map/pallas_call | solution.py:253
  61.0 1.5 %copy.14 = f32[1,16,2,12,512]{4,2,3,1,0:T(2,128)} copy(f32[1,16,2,12,512]{4,3,2,1,0:T(8,128)S(1)} %shard_map.82) | data formatting | bytes 1572864 | tf_op jit(solution)/shard_map/pallas_call | solution.py:253
  (1 shorter events, 0.0 us)
Async XLA Ops:
  4.3 1.0 %copy-start = (bf16[2,16,8192]{2,1,0:T(8,128)(2,1)S(1)}, bf16[2,16,8192]{2,1,0:T(8,128)(2,1)}, u32[]{:S(2)}) copy-start(bf16[2,16,8192]{2,1,0:T(8,128)(2,1)} %volt.1) | copy-start | bytes 1572868
  5.3 1.0 %copy-start.1 = (bf16[512,512]{1,0:T(8,128)(2,1)S(1)}, bf16[512,512]{1,0:T(8,128)(2,1)}, u32[]{:S(2)}) copy-start(bf16[512,512]{1,0:T(8,128)(2,1)} %constant.42.clone.low) | copy-start | bytes 1572868
  6.3 1.0 %copy-start.2 = (bf16[512,512]{1,0:T(8,128)(2,1)S(1)}, bf16[512,512]{1,0:T(8,128)(2,1)}, u32[]{:S(2)}) copy-start(bf16[512,512]{1,0:T(8,128)(2,1)} %constant.41.clone.high) | copy-start | bytes 1572868
  7.4 0.7 %copy-start.3 = (f32[4,1024]{1,0:T(4,128)S(1)}, f32[4,1024]{1,0:T(4,128)}, u32[]{:S(2)}) copy-start(f32[4,1024]{1,0:T(4,128)} %taps.1) | copy-start | bytes 49156
  8.1 0.7 %copy-start.4 = (f32[8,256]{1,0:T(8,128)S(1)}, f32[8,256]{1,0:T(8,128)}, u32[]{:S(2)}) copy-start(f32[8,256]{1,0:T(8,128)} %constant.43.clone.twiddle) | copy-start | bytes 24580

commit v2 on v1

v2 whole, which is shorter than its diff:
```python
import functools
import math

import jax
import jax.numpy as jnp
import numpy as np
from jax import lax
from jax.experimental import pallas as pl
from jax.experimental.pallas import tpu as pltpu
from jax.sharding import PartitionSpec as P

CHANNELS = 1024
TAPS = 4
RADIX = 4
SHORT = CHANNELS // RADIX
CAPACITY = 16
LOCAL = 16
HALF = 4
LANES = 128
GROUP = LANES // CAPACITY
REF_ROWS = 16
DEEP_ROWS = 24
CORES = 2
UNROLL = 8
MESH = pl.DeviceIdType.MESH


def tables():
    n = np.arange(SHORT)
    angle = 2.0 * math.pi * ((n[:, None] * n[None, :]) % SHORT) / SHORT
    cos, sin = np.cos(angle), np.sin(angle)
    full = np.block([[cos, -sin], [sin, cos]]) / math.sqrt(CHANNELS)
    high = full.astype(np.float32).astype(jnp.bfloat16)
    low = (full - high.astype(np.float64)).astype(np.float32).astype(jnp.bfloat16)
    turn = 2.0 * math.pi * np.arange(RADIX)[:, None] * n[None, :] / CHANNELS
    twiddle = np.stack([np.cos(turn), np.sin(turn)], axis=1).reshape(2 * RADIX, SHORT)
    return high, low, twiddle.astype(np.float32)


def kernel(owners, sections, volt_in, taps_in, flagged, owner_row, refs, high_in, low_in, twiddle_in, out,
           volt, taps, high, low, twiddle, column,
           halo, zhi, zlo, stage, onehot, outbox, inbox, refbox, refin, weights,
           load_sem, halo_sem, send_sem, recv_sem, ref_send, ref_recv):
    p, s = lax.axis_index("inp"), lax.axis_index("sec")
    span = owners // sections
    q = lax.div(p, span)
    place = lax.rem(p, span)
    row_count = owners // (GROUP * CORES)
    own_row = lax.div(p, GROUP * CORES)
    own_place = lax.rem(lax.div(p, CORES), GROUP)
    core = lax.rem(p, CORES)

    def holder(b, w, k):
        return (lax.rem(3 * k + b, row_count) * GROUP + k) * CORES + lax.rem(w + k, CORES)
    rows = span * LOCAL
    at_home = q == s

    loads = [
        pltpu.make_async_copy(here, there, load_sem.at[k]) for k, (here, there) in enumerate((
            (volt_in, volt), (taps_in, taps), (twiddle_in, twiddle), (high_in, high), (low_in, low)))]
    for load in loads:
        load.start()
    barrier = pltpu.get_barrier_semaphore()

    def greet(k, carry):
        for t in range(sections):
            pl.semaphore_signal(barrier, inc=1, device_id=(s * span + k, t), device_id_type=MESH)
        return carry
    lax.fori_loop(0, span, greet, 0, unroll=UNROLL)
    for d in range(1, sections):
        pl.semaphore_signal(barrier, inc=1, device_id=(p, lax.rem(s + d, sections)), device_id_type=MESH)

    lane = lax.broadcasted_iota(jnp.int32, (LOCAL, LANES), 1)
    block = lane // CAPACITY

    def spectra(h):
        for b in range(HALF):
            parts = []
            for part in range(2):
                pieces = []
                for n1 in range(RADIX):
                    total = None
                    for t in range(TAPS):
                        frame = h * HALF + b + t
                        if frame < 2 * HALF:
                            source = volt[part, :, pl.ds(frame * CHANNELS + n1 * SHORT, SHORT)].astype(jnp.float32)
                        else:
                            source = halo[part, :, pl.ds((frame - 2 * HALF) * CHANNELS + n1 * SHORT, SHORT)].astype(jnp.float32)
                            source = jnp.where(s == sections - 1, 0.0, source)
                        term = taps[t:t + 1, n1 * SHORT:(n1 + 1) * SHORT] * source
                        total = term if total is None else total + term
                    pieces.append(total)
                parts.append(pieces)
            (r0, r1, r2, r3), (i0, i1, i2, i3) = parts
            ar, ai, br, bi = r0 + r2, i0 + i2, r0 - r2, i0 - i2
            cr, ci, dr, di = r1 + r3, i1 + i3, r1 - r3, i1 - i3
            mixed = [(ar + cr, ai + ci), (br + di, bi - dr), (ar - cr, ai - ci), (br - di, bi + dr)]
            for c1 in range(RADIX):
                re, im = mixed[c1]
                if c1:
                    cos, sin = twiddle[2 * c1:2 * c1 + 1, :], twiddle[2 * c1 + 1:2 * c1 + 2, :]
                    re, im = re * cos + im * sin, im * cos - re * sin
                at = pl.ds((c1 * HALF + b) * LOCAL, LOCAL)
                for k, value in enumerate((re, im)):
                    top = value.astype(jnp.bfloat16)
                    zhi[at, k * SHORT:(k + 1) * SHORT] = top
                    zlo[at, k * SHORT:(k + 1) * SHORT] = (value - top.astype(jnp.float32)).astype(jnp.bfloat16)
        top = zhi[...]
        product = jnp.dot(top, high[...], preferred_element_type=jnp.float32)
        product += jnp.dot(zlo[...], high[...], preferred_element_type=jnp.float32)
        product += jnp.dot(top, low[...], preferred_element_type=jnp.float32)
        product = product.astype(jnp.bfloat16)
        deep = HALF * LOCAL
        for c1 in range(RADIX):
            for part in range(2):
                stage[h, part * deep:(part + 1) * deep, c1 * SHORT:(c1 + 1) * SHORT] = (
                    product[c1 * deep:(c1 + 1) * deep, part * SHORT:(part + 1) * SHORT])

    def place_channels():
        channel = lax.broadcasted_iota(jnp.int32, (1, CHANNELS), 1)
        dropped = channel == flagged[0]
        for k in range(1, flagged.shape[0]):
            dropped = dropped | (channel == flagged[k])
        kept = jnp.where(dropped, -1, owner_row[...]).astype(jnp.float32)
        upper = (lax.broadcasted_iota(jnp.int32, (LANES, LANES), 1)
                 < lax.broadcasted_iota(jnp.int32, (LANES, LANES), 0))
        ones = jnp.ones((LANES, LANES), jnp.bfloat16)
        for a in range(CHANNELS // LANES):
            across = jnp.broadcast_to(kept[:, a * LANES:(a + 1) * LANES], (LANES, LANES))
            own = across.T
            same = jnp.where(upper & (own == across), 1.0, 0.0)
            for e in range(a):
                same += jnp.where(own == kept[:, e * LANES:(e + 1) * LANES], 1.0, 0.0)
            rank = jnp.dot(same.astype(jnp.bfloat16), ones, preferred_element_type=jnp.float32)
            column[a * LANES:(a + 1) * LANES, :] = jnp.where(own < 0.0, -1.0, own * CAPACITY + rank).astype(jnp.int32)

    def build(j, carry):
        base = pl.multiple_of(j * LANES, LANES)
        spot = lax.broadcasted_iota(jnp.int32, (SHORT, LANES), 1)
        slot = holder(lax.div(j, CORES), lax.rem(j, CORES), spot // CAPACITY) * CAPACITY + spot % CAPACITY
        for c1 in range(RADIX):
            hit = column[pl.ds(c1, SHORT, stride=RADIX), :] == slot
            onehot[c1 * SHORT:(c1 + 1) * SHORT, pl.ds(base, LANES)] = jnp.where(hit, 1.0, 0.0).astype(jnp.bfloat16)
        return carry

    def parcel_of(o):
        k = lax.rem(lax.div(o, CORES), GROUP)
        w = lax.rem(lax.rem(o, CORES) + k, CORES)
        b = lax.rem(lax.div(o, CORES * GROUP) + 5 * k, row_count)
        return (b * CORES + w) * GROUP + k

    def around(d, size):
        return min(d % size, size - d % size)

    def far_first():
        landing = inbox.at[1, s, pl.ds(pl.multiple_of(place * LOCAL, LOCAL), LOCAL), :]
        steps = sorted(
            ((dy, dz, dc) for dc in range(CORES) for dy in range(row_count) for dz in range(GROUP)),
            key=lambda d: (-around(d[0], row_count) - around(d[1], GROUP), d[2], d[1], d[0]))
        flip_y = 1 - 2 * lax.rem(s, 2)
        flip_z = 1 - 2 * lax.rem(lax.div(s, 2), 2)
        for dy, dz, dc in steps:
            there_y = lax.rem(own_row + flip_y * dy + row_count, row_count)
            there_z = lax.rem(own_place + flip_z * dz + GROUP, GROUP)
            o = (there_y * GROUP + there_z) * CORES + lax.rem(core + dc, CORES)
            parcel = outbox.at[1, parcel_of(o)]

            def away():
                pltpu.make_async_remote_copy(
                    src_ref=parcel, dst_ref=landing, send_sem=send_sem.at[1],
                    recv_sem=recv_sem.at[1], device_id=(o, q), device_id_type=MESH).start()

            def home():
                pltpu.make_async_copy(parcel, landing, recv_sem.at[1]).start()

            if dy or dz or dc:
                away()
            else:
                pl.when(at_home)(home)
                pl.when(jnp.logical_not(at_home))(away)

    def ship(h):
        landing = inbox.at[h, s, pl.ds(pl.multiple_of(place * LOCAL, LOCAL), LOCAL), :]

        def one_batch(step, carry):
            b = lax.rem(own_row + 5 * own_place + 2 * s + step, row_count)
            base = pl.multiple_of(b * CORES * LANES, CORES * LANES)
            picked = jnp.dot(stage[h], onehot[:, pl.ds(base, CORES * LANES)], preferred_element_type=jnp.float32)
            for w in range(CORES):
                tiles = []
                for k in range(GROUP):
                    tile = picked[k * LOCAL:(k + 1) * LOCAL, w * LANES:(w + 1) * LANES]
                    tiles.append(pltpu.roll(tile, k * CAPACITY, 1) if k else tile)
                for bit in range(3):
                    reach = 1 << bit
                    taken = ((block // reach) % 2) == 1
                    tiles = [jnp.where(taken, tiles[(m + reach) % GROUP], tiles[m]) for m in range(GROUP)]
                for k in range(GROUP):
                    outbox[h, (b * CORES + w) * GROUP + k] = tiles[(GROUP - k) % GROUP].astype(jnp.bfloat16)

            for n in range(CORES * GROUP if h == 0 else 0):
                k = lax.rem(own_place + 1 + n, GROUP)
                w = lax.rem(core + n // GROUP, CORES)
                o = holder(b, w, k)
                parcel = outbox.at[h, (b * CORES + w) * GROUP + k]

                def away():
                    pltpu.make_async_remote_copy(
                        src_ref=parcel, dst_ref=landing, send_sem=send_sem.at[h],
                        recv_sem=recv_sem.at[h], device_id=(o, q), device_id_type=MESH).start()

                def home():
                    pltpu.make_async_copy(parcel, landing, recv_sem.at[h]).start()

                if (1 + n) % GROUP:
                    away()
                else:
                    mine = (o == p) & at_home
                    pl.when(mine)(home)
                    pl.when(jnp.logical_not(mine))(away)
            return carry
        lax.fori_loop(0, row_count, one_batch, 0)
        if h == 1:
            far_first()

    place_channels()
    lax.fori_loop(0, row_count * CORES, build, 0)
    for load in loads:
        load.wait()
    spectra(0)

    pl.semaphore_wait(barrier, owners + sections - 1)

    halo_copy = pltpu.make_async_remote_copy(
        src_ref=volt.at[:, :, pl.ds(0, (TAPS - 1) * CHANNELS)], dst_ref=halo, send_sem=halo_sem.at[0],
        recv_sem=halo_sem.at[1], device_id=(p, lax.rem(s + sections - 1, sections)), device_id_type=MESH)
    halo_copy.start()
    ship(0)
    halo_copy.wait()
    spectra(1)
    ship(1)

    index = lax.broadcasted_iota(jnp.int32, (REF_ROWS, rows), 1) + s * rows
    line = lax.broadcasted_iota(jnp.int32, (REF_ROWS, rows), 0)
    wanted = jnp.full((REF_ROWS, rows), -1, jnp.int32)
    for k in range(refs.shape[0]):
        wanted = jnp.where(line == k, refs[k], wanted)
    chosen = jnp.where(wanted == index, 1.0, 0.0).astype(jnp.bfloat16)

    def gather_refs(h):
        pltpu.make_async_copy(inbox.at[h], inbox.at[h], recv_sem.at[h]).wait()
        for t in range(sections):
            found = jnp.dot(chosen, inbox[h, t], preferred_element_type=jnp.float32)
            refbox[h, t * REF_ROWS:(t + 1) * REF_ROWS, :] = found.astype(jnp.bfloat16)
        copies = []
        for d in range(1, sections):
            copies.append(pltpu.make_async_remote_copy(
                src_ref=refbox.at[h], dst_ref=refin.at[h, d - 1], send_sem=ref_send.at[h, d - 1],
                recv_sem=ref_recv.at[h, d - 1], device_id=(p, lax.rem(s + d, sections)), device_id_type=MESH))
        for copy in copies:
            copy.start()
        return copies

    wide = lax.broadcasted_iota(jnp.int32, (DEEP_ROWS, LANES), 1)
    inner = wide % CAPACITY
    part_of = ((wide // CAPACITY + (GROUP - own_place)) % GROUP) // HALF
    sign = jnp.where(part_of == 1, 1.0, -1.0)
    straight = lax.broadcasted_iota(jnp.int32, (DEEP_ROWS, LANES), 0) % 2 == 0
    spread = jnp.where(
        lax.broadcasted_iota(jnp.int32, (DEEP_ROWS, REF_ROWS), 0) // 2
        == lax.broadcasted_iota(jnp.int32, (DEEP_ROWS, REF_ROWS), 1), 1.0, 0.0).astype(jnp.bfloat16)

    def correlate(h, copies):
        for copy in copies:
            copy.wait()
        pieces, sides = [], []
        for t in range(sections):
            at = pl.ds(t * REF_ROWS, REF_ROWS)
            found = refbox[h, at, :].astype(jnp.float32)
            for d in range(1, sections):
                found += refin[h, d - 1, at, :].astype(jnp.float32)
            pair = jnp.dot(spread, found.astype(jnp.bfloat16), preferred_element_type=jnp.float32)
            both = jnp.where(straight, pair, pltpu.roll(pair, LANES // 2, 1) * sign)
            masked = [jnp.where(inner == k, both, 0.0) for k in range(CAPACITY)]
            pieces.append(jnp.concatenate(masked, axis=0).astype(jnp.bfloat16))
            sides.append(inbox[h, t])
        return lax.dot_general(jnp.concatenate(pieces, axis=1), jnp.concatenate(sides, axis=1),
                               (((1,), (1,)), ((), ())), preferred_element_type=jnp.float32)

    tiles = rows // LANES
    first = gather_refs(0)
    total = correlate(0, first)
    for t in range(tiles):
        weights[t] = total[:, t * LANES:(t + 1) * LANES]
    second = gather_refs(1)
    total = correlate(1, second)
    for t in range(tiles):
        weights[t] = (weights[t] + total[:, t * LANES:(t + 1) * LANES]) * (1.0 / (2 * HALF * sections))
    count = refs.shape[0]
    for k in range(CAPACITY):
        for part in range(2):
            for t in range(tiles):
                start = k * count * tiles * 2 + 2 * t + part
                out[pl.ds(start, count, stride=2 * tiles), :] = weights[
                    t, pl.ds(k * DEEP_ROWS + part, count, stride=2), :]

    for h in range(2):
        @pl.when(at_home)
        def _():
            some = outbox.at[h, pl.ds(0, owners - 1)]
            pltpu.make_async_copy(some, some, send_sem.at[h]).wait()

        @pl.when(jnp.logical_not(at_home))
        def _():
            pltpu.make_async_copy(outbox.at[h], outbox.at[h], send_sem.at[h]).wait()


def on_device(voltages, filter_taps, flagged, channel_owner, ref_inputs):
    owners = lax.axis_size("inp")
    sections = lax.axis_size("sec")
    count = ref_inputs.shape[0]
    high, low, twiddle = tables()
    inputs = owners * LOCAL // sections
    bf16, f32 = jnp.bfloat16, jnp.float32
    vmem = pl.BlockSpec(memory_space=pltpu.VMEM)
    smem = pl.BlockSpec(memory_space=pltpu.SMEM)
    far = pl.BlockSpec(memory_space=pl.ANY)
    flat = pl.pallas_call(
        functools.partial(kernel, owners, sections),
        out_shape=jax.ShapeDtypeStruct((CAPACITY * count * 2 * inputs // LANES, LANES), f32),
        in_specs=[far, far, smem, vmem, smem, far, far, far],
        out_specs=vmem,
        scratch_shapes=[
            pltpu.VMEM(voltages.shape, bf16),
            pltpu.VMEM(filter_taps.shape, f32),
            pltpu.VMEM(high.shape, bf16),
            pltpu.VMEM(low.shape, bf16),
            pltpu.VMEM(twiddle.shape, f32),
            pltpu.VMEM((CHANNELS, LANES), jnp.int32),
            pltpu.VMEM((2, LOCAL, (TAPS - 1) * CHANNELS), bf16),
            pltpu.VMEM((RADIX * HALF * LOCAL, 2 * SHORT), bf16),
            pltpu.VMEM((RADIX * HALF * LOCAL, 2 * SHORT), bf16),
            pltpu.VMEM((2, 2 * HALF * LOCAL, CHANNELS), bf16),
            pltpu.VMEM((CHANNELS, owners * CAPACITY), bf16),
            pltpu.VMEM((2, owners, LOCAL, LANES), bf16),
            pltpu.VMEM((2, sections, inputs, LANES), bf16),
            pltpu.VMEM((2, sections * REF_ROWS, LANES), bf16),
            pltpu.VMEM((2, sections - 1, sections * REF_ROWS, LANES), bf16),
            pltpu.VMEM((inputs // LANES, CAPACITY * DEEP_ROWS, LANES), f32),
            pltpu.SemaphoreType.DMA((5,)),
            pltpu.SemaphoreType.DMA((2,)),
            pltpu.SemaphoreType.DMA((2,)),
            pltpu.SemaphoreType.DMA((2,)),
            pltpu.SemaphoreType.DMA((2, sections - 1)),
            pltpu.SemaphoreType.DMA((2, sections - 1)),
        ],
        compiler_params=pltpu.CompilerParams(
            collective_id=0, has_side_effects=True, vmem_limit_bytes=60 * 1024 * 1024),
    )(voltages, filter_taps, flagged, channel_owner.reshape(1, CHANNELS), ref_inputs,
      jnp.asarray(high), jnp.asarray(low), jnp.asarray(twiddle))
    split = flat.reshape(1, CAPACITY, count, inputs // LANES, 2, LANES)
    return split.transpose(0, 1, 4, 2, 3, 5).reshape(1, CAPACITY, 2, count, inputs)


def solution(mesh):
    return jax.shard_map(
        on_device,
        mesh=mesh,
        in_specs=(P(None, "inp", "sec"), P(), P(), P(), P()),
        out_specs=P("inp", None, None, None, "sec"),
        check_vma=False,
    )
```

time: 63.7 us -> 53.7 us (0.84); the launches traced: 62.5 us -> 53.6 us
  local copies, waits for them, and re-layouts: 6.91 us -> 2.28 us
  other arithmetic: 3.36 us -> 0 us
  Pallas kernels: 52.2 us -> 51.3 us
    unnamed x10 -> x1, local copies, waits for them, and re-layouts: 4.53 us -> 2.28 us
    pallas_call x1 -> x0, local copies, waits for them, and re-layouts: 1.49 us -> none  [on_device(): pl.pallas_call(functools.partial(kernel, owners, sections), out_shape=jax...]
    select_n x2 -> x0, other arithmetic: 1.39 us -> none  [the longest x1 0.69 us: slot_targets(): return jnp.where(dropped, -1, channel_owner * CAPACITY + rank)]
    reduce_sum x1 -> x0, other arithmetic: 1.2 us -> none  [slot_targets(): rank = jnp.sum(earlier.astype(jnp.int32), axis=1)]
    pallas_call x1, Pallas kernels: 52.2 us -> 51.3 us  [on_device(): pl.pallas_call(functools.partial(kernel, owners, sections), out_shape=jax...]
    reduce_or x1 -> x0, other arithmetic: 0.77 us -> none  [slot_targets(): dropped = jnp.any(channel[:, None] == flagged[None, :], axis=1)]
    another operation x1 -> x0, local copies, waits for them, and re-layouts: 0.74 us -> none
where the time goes in v2:
time: 53.7 us; the launch traced here: 53.6 us
  Pallas kernels  51.3 us (96%)
  local copies, waits for them, and re-layouts  2.28 us (4%)
    pallas_call x1, Pallas kernels, on_device(): pl.pallas_call(functools.partial(kernel, owners, sections), out_shape=jax...  51.3 us
    unnamed x1, local copies, waits for them, and re-layouts  2.28 us

profile of v2, /device:TPU:1, one launch (start us, length us, event | category | flops | bytes accessed | tf_op | source)
XLA Modules:
  0.0 53.6 jit_solution(7416537407217393332)
XLA Ops:
  0.0 51.3 %shard_map.82 = f32[1536,128]{1,0:T(8,128)} custom-call(bf16[2,16,8192]{2,1,0:T(8,128)(2,1)} %volt_in.1, f32[4,1024]{1,0:T(4,128)} %taps_in.1, s32[64]{0:T(128)} %flagged.1, s32[1,1024]{1,0:T(1,128)} %bitcast.7, s32[12]{0:T(128)} %refs.1, bf16[512,512]{1,0:T(8,128)(2,1)} %constant.6.clone.high_in, bf16[512,512]{1,0:T(8,128)(2,1)} %constant.7.clone.low_in, ...), custom_call_target="tpu_custom_call" | custom-call | tf_op jit(solution)/shard_map/pallas_call | solution.py:328
  51.3 2.3 %copy.11 = f32[1,16,2,12,512]{4,2,3,1,0:T(2,128)} copy(f32[1,16,2,12,512]{4,2,3,1,0:T(2,128)} %bitcast.6) | data formatting | bytes 1572864

commit v3 on v2

--- a/solution.py
+++ b/solution.py
@@ -19,9 +19,9 @@
 LANES = 128
 GROUP = LANES // CAPACITY
 REF_ROWS = 16
-DEEP_ROWS = 24
 CORES = 2
 UNROLL = 8
+SAVES = 2
 MESH = pl.DeviceIdType.MESH
 
 
@@ -37,10 +37,10 @@
     return high, low, twiddle.astype(np.float32)
 
 
-def kernel(owners, sections, volt_in, taps_in, flagged, owner_row, refs, high_in, low_in, twiddle_in, out,
+def kernel(owners, sections, volt_in, taps_in, flagged, owner_row, refs, high_in, low_in, twiddle_in, inbox_out, refs_out,
            volt, taps, high, low, twiddle, column,
-           halo, zhi, zlo, stage, onehot, outbox, inbox, refbox, refin, weights,
-           load_sem, halo_sem, send_sem, recv_sem, ref_send, ref_recv):
+           halo, zhi, zlo, stage, onehot, outbox, inbox, refbox,
+           load_sem, save_sem, halo_sem, send_sem, recv_sem, ref_send, ref_recv):
     p, s = lax.axis_index("inp"), lax.axis_index("sec")
     span = owners // sections
     q = lax.div(p, span)
@@ -249,60 +249,24 @@
 
     def gather_refs(h):
         pltpu.make_async_copy(inbox.at[h], inbox.at[h], recv_sem.at[h]).wait()
-        for t in range(sections):
-            found = jnp.dot(chosen, inbox[h, t], preferred_element_type=jnp.float32)
-            refbox[h, t * REF_ROWS:(t + 1) * REF_ROWS, :] = found.astype(jnp.bfloat16)
+        side = jnp.concatenate([inbox[h, t] for t in range(sections)], axis=1)
+        refbox[h] = jnp.dot(chosen, side, preferred_element_type=jnp.float32).astype(jnp.bfloat16)
         copies = []
         for d in range(1, sections):
             copies.append(pltpu.make_async_remote_copy(
-                src_ref=refbox.at[h], dst_ref=refin.at[h, d - 1], send_sem=ref_send.at[h, d - 1],
+                src_ref=refbox.at[h], dst_ref=refs_out.at[h, d], send_sem=ref_send.at[h, d - 1],
                 recv_sem=ref_recv.at[h, d - 1], device_id=(p, lax.rem(s + d, sections)), device_id_type=MESH))
+        copies.append(pltpu.make_async_copy(refbox.at[h], refs_out.at[h, 0], save_sem.at[2 + h]))
         for copy in copies:
             copy.start()
+        copies.append(pltpu.make_async_copy(inbox.at[h], inbox_out.at[h], save_sem.at[h]))
+        copies[-1].start()
         return copies
 
-    wide = lax.broadcasted_iota(jnp.int32, (DEEP_ROWS, LANES), 1)
-    inner = wide % CAPACITY
-    part_of = ((wide // CAPACITY + (GROUP - own_place)) % GROUP) // HALF
-    sign = jnp.where(part_of == 1, 1.0, -1.0)
-    straight = lax.broadcasted_iota(jnp.int32, (DEEP_ROWS, LANES), 0) % 2 == 0
-    spread = jnp.where(
-        lax.broadcasted_iota(jnp.int32, (DEEP_ROWS, REF_ROWS), 0) // 2
-        == lax.broadcasted_iota(jnp.int32, (DEEP_ROWS, REF_ROWS), 1), 1.0, 0.0).astype(jnp.bfloat16)
-
-    def correlate(h, copies):
-        for copy in copies:
+    copies = [gather_refs(0), gather_refs(1)]
+    for h in range(2):
+        for copy in copies[h]:
             copy.wait()
-        pieces, sides = [], []
-        for t in range(sections):
-            at = pl.ds(t * REF_ROWS, REF_ROWS)
-            found = refbox[h, at, :].astype(jnp.float32)
-            for d in range(1, sections):
-                found += refin[h, d - 1, at, :].astype(jnp.float32)
-            pair = jnp.dot(spread, found.astype(jnp.bfloat16), preferred_element_type=jnp.float32)
-            both = jnp.where(straight, pair, pltpu.roll(pair, LANES // 2, 1) * sign)
-            masked = [jnp.where(inner == k, both, 0.0) for k in range(CAPACITY)]
-            pieces.append(jnp.concatenate(masked, axis=0).astype(jnp.bfloat16))
-            sides.append(inbox[h, t])
-        return lax.dot_general(jnp.concatenate(pieces, axis=1), jnp.concatenate(sides, axis=1),
-                               (((1,), (1,)), ((), ())), preferred_element_type=jnp.float32)
-
-    tiles = rows // LANES
-    first = gather_refs(0)
-    total = correlate(0, first)
-    for t in range(tiles):
-        weights[t] = total[:, t * LANES:(t + 1) * LANES]
-    second = gather_refs(1)
-    total = correlate(1, second)
-    for t in range(tiles):
-        weights[t] = (weights[t] + total[:, t * LANES:(t + 1) * LANES]) * (1.0 / (2 * HALF * sections))
-    count = refs.shape[0]
-    for k in range(CAPACITY):
-        for part in range(2):
-            for t in range(tiles):
-                start = k * count * tiles * 2 + 2 * t + part
-                out[pl.ds(start, count, stride=2 * tiles), :] = weights[
-                    t, pl.ds(k * DEEP_ROWS + part, count, stride=2), :]
 
     for h in range(2):
         @pl.when(at_home)
@@ -313,6 +277,80 @@
         @pl.when(jnp.logical_not(at_home))
         def _():
             pltpu.make_async_copy(outbox.at[h], outbox.at[h], send_sem.at[h]).wait()
+
+
+def correlate(sections, count, found_in, inbox_in, out_far, found, inbox, out, load_sem, save_sem):
+    p = lax.axis_index("inp")
+    place = lax.rem(lax.div(p, CORES), GROUP)
+    loads = [pltpu.make_async_copy(found_in, found, load_sem.at[2])]
+    loads += [pltpu.make_async_copy(inbox_in.at[h], inbox.at[h], load_sem.at[h]) for h in range(2)]
+    for load in loads:
+        load.start()
+    lane = lax.broadcasted_iota(jnp.int32, (REF_ROWS, LANES), 1)
+    part_of = ((lane // CAPACITY + (GROUP - place)) % GROUP) // HALF
+    sign = jnp.where(part_of == 1, 1.0, -1.0)
+    height = count * 2 * CAPACITY
+    line = lax.broadcasted_iota(jnp.int32, (height, 2 * REF_ROWS), 0)
+    some = CAPACITY // SAVES
+    source = lax.rem(lax.div(line, 2 * some), count) + REF_ROWS * lax.rem(lax.div(line, some), 2)
+    spread = jnp.where(source == lax.broadcasted_iota(jnp.int32, (height, 2 * REF_ROWS), 1), 1.0, 0.0)
+    spread = spread.astype(jnp.bfloat16)
+    loads[0].wait()
+    pieces = []
+    for h in range(2):
+        total = found[h, 0].astype(jnp.float32)
+        for d in range(1, sections):
+            total += found[h, d].astype(jnp.float32)
+        turned = [pltpu.roll(total[:, t * LANES:(t + 1) * LANES], LANES // 2, 1) * sign for t in range(sections)]
+        pieces.append(jnp.concatenate([total, jnp.concatenate(turned, axis=1)], axis=0).astype(jnp.bfloat16))
+    both = jnp.concatenate(pieces, axis=1)
+    weights = jnp.dot(spread, both, preferred_element_type=jnp.float32)
+    line = lax.broadcasted_iota(jnp.int32, weights.shape, 0)
+    slot = lax.rem(line, some) + some * lax.div(line, 2 * count * some)
+    keep = slot == lax.broadcasted_iota(jnp.int32, weights.shape, 1) % CAPACITY
+    weights = jnp.where(keep, weights, 0.0).astype(jnp.bfloat16)
+    for load in loads[1:]:
+        load.wait()
+    side = jnp.concatenate([inbox[h, t] for h in range(2) for t in range(sections)], axis=1)
+    tiles = side.shape[0] // LANES
+    saves = []
+    share = 2 * count * some
+    deep = 2 * count * tiles
+    product = lax.dot_general(weights, side, (((1,), (1,)), ((), ())), preferred_element_type=jnp.float32)
+    product = product * (1.0 / (2 * HALF * sections))
+    for a in range(SAVES):
+        total = product[a * share:(a + 1) * share, :]
+        for r in range(count):
+            for part in range(2):
+                piece = total[(2 * r + part) * some:(2 * r + part + 1) * some, :]
+                for t in range(tiles):
+                    out[pl.ds(a * some * deep + (r * tiles + t) * 2 + part, some, stride=deep), :] = (
+                        piece[:, t * LANES:(t + 1) * LANES])
+        at = pl.ds(a * some * deep, some * deep)
+        saves.append(pltpu.make_async_copy(out.at[at], out_far.at[at], save_sem.at[a]))
+        saves[-1].start()
+    for save in saves:
+        save.wait()
+
+
+def finish(sections, count, inputs, found, arrived):
+    bf16, f32 = jnp.bfloat16, jnp.float32
+    far = pl.BlockSpec(memory_space=pl.ANY)
+    height = CAPACITY * count * 2 * inputs // LANES
+    return pl.pallas_call(
+        functools.partial(correlate, sections, count),
+        out_shape=jax.ShapeDtypeStruct((height, LANES), f32),
+        in_specs=[far, far],
+        out_specs=far,
+        scratch_shapes=[
+            pltpu.VMEM(found.shape, bf16),
+            pltpu.VMEM(arrived.shape, bf16),
+            pltpu.VMEM((height, LANES), f32),
+            pltpu.SemaphoreType.DMA((3,)),
+            pltpu.SemaphoreType.DMA((SAVES,)),
+        ],
+        compiler_params=pltpu.CompilerParams(vmem_limit_bytes=60 * 1024 * 1024),
+    )(found, arrived)
 
 
 def on_device(voltages, filter_taps, flagged, channel_owner, ref_inputs):
@@ -325,11 +363,14 @@
     vmem = pl.BlockSpec(memory_space=pltpu.VMEM)
     smem = pl.BlockSpec(memory_space=pltpu.SMEM)
     far = pl.BlockSpec(memory_space=pl.ANY)
-    flat = pl.pallas_call(
+    arrived, found = pl.pallas_call(
         functools.partial(kernel, owners, sections),
-        out_shape=jax.ShapeDtypeStruct((CAPACITY * count * 2 * inputs // LANES, LANES), f32),
+        out_shape=(
+            jax.ShapeDtypeStruct((2, sections, inputs, LANES), bf16),
+            jax.ShapeDtypeStruct((2, sections, REF_ROWS, sections * LANES), bf16),
+        ),
         in_specs=[far, far, smem, vmem, smem, far, far, far],
-        out_specs=vmem,
+        out_specs=(far, far),
         scratch_shapes=[
             pltpu.VMEM(voltages.shape, bf16),
             pltpu.VMEM(filter_taps.shape, f32),
@@ -344,10 +385,9 @@
             pltpu.VMEM((CHANNELS, owners * CAPACITY), bf16),
             pltpu.VMEM((2, owners, LOCAL, LANES), bf16),
             pltpu.VMEM((2, sections, inputs, LANES), bf16),
-            pltpu.VMEM((2, sections * REF_ROWS, LANES), bf16),
-            pltpu.VMEM((2, sections - 1, sections * REF_ROWS, LANES), bf16),
-            pltpu.VMEM((inputs // LANES, CAPACITY * DEEP_ROWS, LANES), f32),
+            pltpu.VMEM((2, REF_ROWS, sections * LANES), bf16),
             pltpu.SemaphoreType.DMA((5,)),
+            pltpu.SemaphoreType.DMA((4,)),
             pltpu.SemaphoreType.DMA((2,)),
             pltpu.SemaphoreType.DMA((2,)),
             pltpu.SemaphoreType.DMA((2,)),
@@ -358,6 +398,7 @@
             collective_id=0, has_side_effects=True, vmem_limit_bytes=60 * 1024 * 1024),
     )(voltages, filter_taps, flagged, channel_owner.reshape(1, CHANNELS), ref_inputs,
       jnp.asarray(high), jnp.asarray(low), jnp.asarray(twiddle))
+    flat = finish(sections, count, inputs, found, arrived)
     split = flat.reshape(1, CAPACITY, count, inputs // LANES, 2, LANES)
     return split.transpose(0, 1, 4, 2, 3, 5).reshape(1, CAPACITY, 2, count, inputs)
 

time: 53.7 us -> 53.2 us (level)
  local copies, waits for them, and re-layouts: 2.28 us -> 0 us
  Pallas kernels: 51.3 us -> 53 us
    unnamed x1 -> x0, local copies, waits for them, and re-layouts: 2.28 us -> none
    pallas_call x1 -> x2, Pallas kernels: 51.3 us -> 53 us  [the longest x1 49.9 us: on_device(): pl.pallas_call(functools.partial(kernel, owners, sections), out_shape=(ja...]
where the time goes in v3:
time: 53.2 us; the launch traced here: 53 us
  Pallas kernels  53 us (100%)
    pallas_call x1, Pallas kernels, on_device(): pl.pallas_call(functools.partial(kernel, owners, sections), out_shape=(ja...  49.9 us
    pallas_call x1, Pallas kernels, finish(): pl.pallas_call(functools.partial(correlate, sections, count), out_shape=j...  3.11 us

profile of v3, /device:TPU:1, one launch (start us, length us, event | category | flops | bytes accessed | tf_op | source)
XLA Modules:
  0.0 53.0 jit_solution(18410774826370812310)
XLA Ops:
  0.0 49.9 %shard_map.82 = (bf16[2,4,512,128]{3,2,1,0:T(8,128)(2,1)}, bf16[2,4,16,512]{3,2,1,0:T(8,128)(2,1)}) custom-call(bf16[2,16,8192]{2,1,0:T(8,128)(2,1)} %volt_in.1, f32[4,1024]{1,0:T(4,128)} %taps_in.1, s32[64]{0:T(128)} %flagged.1, s32[1,1024]{1,0:T(1,128)} %bitcast.6, s32[12]{0:T(128)} %refs.1, bf16[512,512]{1,0:T(8,128)(2,1)} %constant.6.clone.high_in, ...), custom_call_target="tpu_custom_call" | custom-call | tf_op jit(solution)/shard_map/pallas_call | solution.py:366
  49.9 3.1 %shard_map.83 = f32[1536,128]{1,0:T(8,128)} custom-call(bf16[2,4,16,512]{3,2,1,0:T(8,128)(2,1)} %get-tuple-element.7.found_in, bf16[2,4,512,128]{3,2,1,0:T(8,128)(2,1)} %get-tuple-element.8.inbox_in), custom_call_target="tpu_custom_call" | custom-call | tf_op jit(solution)/shard_map/pallas_call | solution.py:340

commit v4 on v3

--- a/solution.py
+++ b/solution.py
@@ -37,8 +37,8 @@
     return high, low, twiddle.astype(np.float32)
 
 
-def kernel(owners, sections, volt_in, taps_in, flagged, owner_row, refs, high_in, low_in, twiddle_in, inbox_out, refs_out,
-           volt, taps, high, low, twiddle, column,
+def kernel(owners, sections, volt_in, taps_in, flagged_in, owner_in, refs_in, high_in, low_in, twiddle_in, inbox_out, refs_out,
+           volt, taps, flagged, owner_row, refs, high, low, twiddle, column,
            halo, zhi, zlo, stage, onehot, outbox, inbox, refbox,
            load_sem, save_sem, halo_sem, send_sem, recv_sem, ref_send, ref_recv):
     p, s = lax.axis_index("inp"), lax.axis_index("sec")
@@ -57,7 +57,8 @@
 
     loads = [
         pltpu.make_async_copy(here, there, load_sem.at[k]) for k, (here, there) in enumerate((
-            (volt_in, volt), (taps_in, taps), (twiddle_in, twiddle), (high_in, high), (low_in, low)))]
+            (flagged_in, flagged), (owner_in, owner_row), (refs_in, refs), (volt_in, volt), (taps_in, taps),
+            (twiddle_in, twiddle), (high_in, high), (low_in, low)))]
     for load in loads:
         load.start()
     barrier = pltpu.get_barrier_semaphore()
@@ -223,9 +224,11 @@
         if h == 1:
             far_first()
 
+    for load in loads[:3]:
+        load.wait()
     place_channels()
     lax.fori_loop(0, row_count * CORES, build, 0)
-    for load in loads:
+    for load in loads[3:]:
         load.wait()
     spectra(0)
 
@@ -360,8 +363,6 @@
     high, low, twiddle = tables()
     inputs = owners * LOCAL // sections
     bf16, f32 = jnp.bfloat16, jnp.float32
-    vmem = pl.BlockSpec(memory_space=pltpu.VMEM)
-    smem = pl.BlockSpec(memory_space=pltpu.SMEM)
     far = pl.BlockSpec(memory_space=pl.ANY)
     arrived, found = pl.pallas_call(
         functools.partial(kernel, owners, sections),
@@ -369,11 +370,14 @@
             jax.ShapeDtypeStruct((2, sections, inputs, LANES), bf16),
             jax.ShapeDtypeStruct((2, sections, REF_ROWS, sections * LANES), bf16),
         ),
-        in_specs=[far, far, smem, vmem, smem, far, far, far],
+        in_specs=[far] * 8,
         out_specs=(far, far),
         scratch_shapes=[
             pltpu.VMEM(voltages.shape, bf16),
             pltpu.VMEM(filter_taps.shape, f32),
+            pltpu.SMEM(flagged.shape, jnp.int32),
+            pltpu.VMEM((1, CHANNELS), jnp.int32),
+            pltpu.SMEM(ref_inputs.shape, jnp.int32),
             pltpu.VMEM(high.shape, bf16),
             pltpu.VMEM(low.shape, bf16),
             pltpu.VMEM(twiddle.shape, f32),
@@ -386,7 +390,7 @@
             pltpu.VMEM((2, owners, LOCAL, LANES), bf16),
             pltpu.VMEM((2, sections, inputs, LANES), bf16),
             pltpu.VMEM((2, REF_ROWS, sections * LANES), bf16),
-            pltpu.SemaphoreType.DMA((5,)),
+            pltpu.SemaphoreType.DMA((8,)),
             pltpu.SemaphoreType.DMA((4,)),
             pltpu.SemaphoreType.DMA((2,)),
             pltpu.SemaphoreType.DMA((2,)),

time: 53.2 us -> 52.3 us (0.983)
  Pallas kernels: 53 us -> 52.2 us
    pallas_call x1, Pallas kernels: 49.9 us -> 49.1 us  [on_device(): pl.pallas_call(functools.partial(kernel, owners, sections), out_shape=(ja...]
where the time goes in v4:
time: 52.3 us; the launch traced here: 52.2 us
  Pallas kernels  52.2 us (100%)
    pallas_call x1, Pallas kernels, on_device(): pl.pallas_call(functools.partial(kernel, owners, sections), out_shape=(ja...  49.1 us
    pallas_call x1, Pallas kernels, finish(): pl.pallas_call(functools.partial(correlate, sections, count), out_shape=j...  3.11 us

profile of v4, /device:TPU:1, one launch (start us, length us, event | category | flops | bytes accessed | tf_op | source)
XLA Modules:
  0.0 52.2 jit_solution(5555667252379028041)
XLA Ops:
  0.0 49.1 %shard_map.82 = (bf16[2,4,512,128]{3,2,1,0:T(8,128)(2,1)}, bf16[2,4,16,512]{3,2,1,0:T(8,128)(2,1)}) custom-call(bf16[2,16,8192]{2,1,0:T(8,128)(2,1)} %volt_in.1, f32[4,1024]{1,0:T(4,128)} %taps_in.1, s32[64]{0:T(128)} %flagged_in.1, s32[1,1024]{1,0:T(1,128)} %bitcast.6, s32[12]{0:T(128)} %refs_in.1, bf16[512,512]{1,0:T(8,128)(2,1)} %constant.6.clone.high_in, ...), custom_call_target="tpu_custom_call" | custom-call | tf_op jit(solution)/shard_map/pallas_call | solution.py:367
  49.1 3.1 %shard_map.83 = f32[1536,128]{1,0:T(8,128)} custom-call(bf16[2,4,16,512]{3,2,1,0:T(8,128)(2,1)} %get-tuple-element.7.found_in, bf16[2,4,512,128]{3,2,1,0:T(8,128)(2,1)} %get-tuple-element.8.inbox_in), custom_call_target="tpu_custom_call" | custom-call | tf_op jit(solution)/shard_map/pallas_call | solution.py:343

commit v5 on v4

--- a/solution.py
+++ b/solution.py
@@ -37,9 +37,9 @@
     return high, low, twiddle.astype(np.float32)
 
 
-def kernel(owners, sections, volt_in, taps_in, flagged_in, owner_in, refs_in, high_in, low_in, twiddle_in, inbox_out, refs_out,
+def kernel(owners, sections, volt_in, taps_in, flagged_in, owner_in, refs_in, high_in, low_in, twiddle_in, inbox_out, refs_out, begun_out,
            volt, taps, flagged, owner_row, refs, high, low, twiddle, column,
-           halo, zhi, zlo, stage, onehot, outbox, inbox, refbox,
+           halo, zhi, zlo, stage, onehot, outbox, inbox, refbox, early, begun,
            load_sem, save_sem, halo_sem, send_sem, recv_sem, ref_send, ref_recv):
     p, s = lax.axis_index("inp"), lax.axis_index("sec")
     span = owners // sections
@@ -262,14 +262,22 @@
         copies.append(pltpu.make_async_copy(refbox.at[h], refs_out.at[h, 0], save_sem.at[2 + h]))
         for copy in copies:
             copy.start()
-        copies.append(pltpu.make_async_copy(inbox.at[h], inbox_out.at[h], save_sem.at[h]))
-        copies[-1].start()
+        if h == 1:
+            copies.append(pltpu.make_async_copy(inbox.at[h], inbox_out, save_sem.at[0]))
+            copies[-1].start()
         return copies
 
-    copies = [gather_refs(0), gather_refs(1)]
-    for h in range(2):
-        for copy in copies[h]:
-            copy.wait()
+    for copy in gather_refs(0):
+        copy.wait()
+    fetch = pltpu.make_async_copy(refs_out.at[0], early, save_sem.at[1])
+    fetch.start()
+    fetch.wait()
+    begun[...] = half_product(sections, refs.shape[0], own_place, early, lambda: [inbox[0, t] for t in range(sections)])
+    keep_half = pltpu.make_async_copy(begun, begun_out, save_sem.at[4])
+    keep_half.start()
+    for copy in gather_refs(1):
+        copy.wait()
+    keep_half.wait()
 
     for h in range(2):
         @pl.when(at_home)
@@ -282,45 +290,48 @@
             pltpu.make_async_copy(outbox.at[h], outbox.at[h], send_sem.at[h]).wait()
 
 
-def correlate(sections, count, found_in, inbox_in, out_far, found, inbox, out, load_sem, save_sem):
-    p = lax.axis_index("inp")
-    place = lax.rem(lax.div(p, CORES), GROUP)
-    loads = [pltpu.make_async_copy(found_in, found, load_sem.at[2])]
-    loads += [pltpu.make_async_copy(inbox_in.at[h], inbox.at[h], load_sem.at[h]) for h in range(2)]
-    for load in loads:
-        load.start()
+def half_product(sections, count, place, found, sides):
     lane = lax.broadcasted_iota(jnp.int32, (REF_ROWS, LANES), 1)
     part_of = ((lane // CAPACITY + (GROUP - place)) % GROUP) // HALF
     sign = jnp.where(part_of == 1, 1.0, -1.0)
     height = count * 2 * CAPACITY
+    some = CAPACITY // SAVES
     line = lax.broadcasted_iota(jnp.int32, (height, 2 * REF_ROWS), 0)
-    some = CAPACITY // SAVES
     source = lax.rem(lax.div(line, 2 * some), count) + REF_ROWS * lax.rem(lax.div(line, some), 2)
     spread = jnp.where(source == lax.broadcasted_iota(jnp.int32, (height, 2 * REF_ROWS), 1), 1.0, 0.0)
-    spread = spread.astype(jnp.bfloat16)
-    loads[0].wait()
-    pieces = []
-    for h in range(2):
-        total = found[h, 0].astype(jnp.float32)
-        for d in range(1, sections):
-            total += found[h, d].astype(jnp.float32)
-        turned = [pltpu.roll(total[:, t * LANES:(t + 1) * LANES], LANES // 2, 1) * sign for t in range(sections)]
-        pieces.append(jnp.concatenate([total, jnp.concatenate(turned, axis=1)], axis=0).astype(jnp.bfloat16))
-    both = jnp.concatenate(pieces, axis=1)
-    weights = jnp.dot(spread, both, preferred_element_type=jnp.float32)
+    total = found[0].astype(jnp.float32)
+    for d in range(1, sections):
+        total += found[d].astype(jnp.float32)
+    turned = [pltpu.roll(total[:, t * LANES:(t + 1) * LANES], LANES // 2, 1) * sign for t in range(sections)]
+    both = jnp.concatenate([total, jnp.concatenate(turned, axis=1)], axis=0).astype(jnp.bfloat16)
+    weights = jnp.dot(spread.astype(jnp.bfloat16), both, preferred_element_type=jnp.float32)
     line = lax.broadcasted_iota(jnp.int32, weights.shape, 0)
     slot = lax.rem(line, some) + some * lax.div(line, 2 * count * some)
     keep = slot == lax.broadcasted_iota(jnp.int32, weights.shape, 1) % CAPACITY
     weights = jnp.where(keep, weights, 0.0).astype(jnp.bfloat16)
-    for load in loads[1:]:
-        load.wait()
-    side = jnp.concatenate([inbox[h, t] for h in range(2) for t in range(sections)], axis=1)
-    tiles = side.shape[0] // LANES
+    side = jnp.concatenate(sides(), axis=1)
+    return lax.dot_general(weights, side, (((1,), (1,)), ((), ())), preferred_element_type=jnp.float32)
+
+
+def correlate(sections, count, found_in, inbox_in, begun_in, out_far, found, inbox, begun, out, load_sem, save_sem):
+    place = lax.rem(lax.div(lax.axis_index("inp"), CORES), GROUP)
+    loads = [pltpu.make_async_copy(here, there, load_sem.at[k]) for k, (here, there) in enumerate((
+        (found_in.at[1], found), (inbox_in, inbox), (begun_in, begun)))]
+    for load in loads:
+        load.start()
+    loads[0].wait()
+
+    def sides():
+        loads[1].wait()
+        return [inbox[t] for t in range(sections)]
+    product = half_product(sections, count, place, found, sides)
+    loads[2].wait()
+    product = (product + begun[...]) * (1.0 / (2 * HALF * sections))
+    tiles = inbox.shape[1] // LANES
     saves = []
+    some = CAPACITY // SAVES
     share = 2 * count * some
     deep = 2 * count * tiles
-    product = lax.dot_general(weights, side, (((1,), (1,)), ((), ())), preferred_element_type=jnp.float32)
-    product = product * (1.0 / (2 * HALF * sections))
     for a in range(SAVES):
         total = product[a * share:(a + 1) * share, :]
         for r in range(count):
@@ -336,24 +347,25 @@
         save.wait()
 
 
-def finish(sections, count, inputs, found, arrived):
+def finish(sections, count, inputs, found, arrived, begun):
     bf16, f32 = jnp.bfloat16, jnp.float32
     far = pl.BlockSpec(memory_space=pl.ANY)
     height = CAPACITY * count * 2 * inputs // LANES
     return pl.pallas_call(
         functools.partial(correlate, sections, count),
         out_shape=jax.ShapeDtypeStruct((height, LANES), f32),
-        in_specs=[far, far],
+        in_specs=[far] * 3,
         out_specs=far,
         scratch_shapes=[
-            pltpu.VMEM(found.shape, bf16),
+            pltpu.VMEM(found.shape[1:], bf16),
             pltpu.VMEM(arrived.shape, bf16),
+            pltpu.VMEM(begun.shape, f32),
             pltpu.VMEM((height, LANES), f32),
             pltpu.SemaphoreType.DMA((3,)),
             pltpu.SemaphoreType.DMA((SAVES,)),
         ],
         compiler_params=pltpu.CompilerParams(vmem_limit_bytes=60 * 1024 * 1024),
-    )(found, arrived)
+    )(found, arrived, begun)
 
 
 def on_device(voltages, filter_taps, flagged, channel_owner, ref_inputs):
@@ -364,14 +376,15 @@
     inputs = owners * LOCAL // sections
     bf16, f32 = jnp.bfloat16, jnp.float32
     far = pl.BlockSpec(memory_space=pl.ANY)
-    arrived, found = pl.pallas_call(
+    arrived, found, begun = pl.pallas_call(
         functools.partial(kernel, owners, sections),
         out_shape=(
-            jax.ShapeDtypeStruct((2, sections, inputs, LANES), bf16),
+            jax.ShapeDtypeStruct((sections, inputs, LANES), bf16),
             jax.ShapeDtypeStruct((2, sections, REF_ROWS, sections * LANES), bf16),
+            jax.ShapeDtypeStruct((count * 2 * CAPACITY, inputs), f32),
         ),
         in_specs=[far] * 8,
-        out_specs=(far, far),
+        out_specs=(far, far, far),
         scratch_shapes=[
             pltpu.VMEM(voltages.shape, bf16),
             pltpu.VMEM(filter_taps.shape, f32),
@@ -390,8 +403,10 @@
             pltpu.VMEM((2, owners, LOCAL, LANES), bf16),
             pltpu.VMEM((2, sections, inputs, LANES), bf16),
             pltpu.VMEM((2, REF_ROWS, sections * LANES), bf16),
+            pltpu.VMEM((sections, REF_ROWS, sections * LANES), bf16),
+            pltpu.VMEM((count * 2 * CAPACITY, inputs), f32),
             pltpu.SemaphoreType.DMA((8,)),
-            pltpu.SemaphoreType.DMA((4,)),
+            pltpu.SemaphoreType.DMA((5,)),
             pltpu.SemaphoreType.DMA((2,)),
             pltpu.SemaphoreType.DMA((2,)),
             pltpu.SemaphoreType.DMA((2,)),
@@ -402,7 +417,7 @@
             collective_id=0, has_side_effects=True, vmem_limit_bytes=60 * 1024 * 1024),
     )(voltages, filter_taps, flagged, channel_owner.reshape(1, CHANNELS), ref_inputs,
       jnp.asarray(high), jnp.asarray(low), jnp.asarray(twiddle))
-    flat = finish(sections, count, inputs, found, arrived)
+    flat = finish(sections, count, inputs, found, arrived, begun)
     split = flat.reshape(1, CAPACITY, count, inputs // LANES, 2, LANES)
     return split.transpose(0, 1, 4, 2, 3, 5).reshape(1, CAPACITY, 2, count, inputs)
 

time: 52.3 us -> 52.2 us (level)
  no operation moved by 1% of the time
where the time goes in v5:
time: 52.2 us; the launch traced here: 52 us
  Pallas kernels  52 us (100%)
    pallas_call x1, Pallas kernels, on_device(): pl.pallas_call(functools.partial(kernel, owners, sections), out_shape=(ja...  49.1 us
    pallas_call x1, Pallas kernels, finish(): pl.pallas_call(functools.partial(correlate, sections, count), out_shape=j...  2.9 us

profile of v5, /device:TPU:1, one launch (start us, length us, event | category | flops | bytes accessed | tf_op | source)
XLA Modules:
  0.0 52.0 jit_solution(16465435508720495801)
XLA Ops:
  0.0 49.1 %shard_map.82 = (bf16[4,512,128]{2,1,0:T(8,128)(2,1)}, bf16[2,4,16,512]{3,2,1,0:T(8,128)(2,1)}, f32[384,512]{1,0:T(8,128)}) custom-call(bf16[2,16,8192]{2,1,0:T(8,128)(2,1)} %volt_in.1, f32[4,1024]{1,0:T(4,128)} %taps_in.1, s32[64]{0:T(128)} %flagged_in.1, s32[1,1024]{1,0:T(1,128)} %bitcast.6, s32[12]{0:T(128)} %refs_in.1, ...), custom_call_target="tpu_custom_call" | custom-call | tf_op jit(solution)/shard_map/pallas_call | solution.py:379
  49.1 2.9 %shard_map.83 = f32[1536,128]{1,0:T(8,128)} custom-call(bf16[2,4,16,512]{3,2,1,0:T(8,128)(2,1)} %get-tuple-element.8.found_in, bf16[4,512,128]{2,1,0:T(8,128)(2,1)} %get-tuple-element.9.inbox_in, f32[384,512]{1,0:T(8,128)} %get-tuple-element.10.begun_in), custom_call_target="tpu_custom_call" | custom-call | tf_op jit(solution)/shard_map/pallas_call | solution.py:354
